TPU v7x, 256 devices: a whole 4x4x8 slice. The times are simulated.
256 devices in a mesh: sub: 64 (over z, y, x_lo), fold: 4 (over x_hi, core).
Axes of the slice: x: 4 (x_hi: 2, x_lo: 2; x = x_hi * 2 + x_lo), y: 4, z: 8, core: 2. Of those that a mesh axis runs over, the one named last changes fastest.
Arguments:
- right_side: float32 [32768, 64], P(('sub', 'fold')), may hold values from -6 to 6
- blocks: float32 [256, 7, 128, 128], P('sub'), may hold values from -2 to 9, as said below
- block_cols: int32 [256, 7], P('sub'), may hold values from 0 to 7, as said below
- send_lists: int32 [64, 2, 2], P('sub'), may hold values from 0 to 3, as said below
Outputs:
- correction: float32 [32768, 64], P(('sub', 'fold'))
- residual: float32 [32768, 64], P(('sub', 'fold'))
Inputs may be any that keep to these rules, and one draw needn't show every extreme that they name: `block_cols`: entry 0 of each block row is the row's own block (its device index). Values below 4 name the device's own blocks, 4 + j the j-th block of the previous device's list to its next neighbour, 6 + j the j-th block of the next device's list to its previous neighbour; the first subset device names no previous neighbour's block and the last none of the next. `send_lists`: each list holds 2 distinct block indices of the device's own blocks. `blocks`: the operator is nonsingular and well conditioned.
All inputs are finite; a program needn't handle non-finite values.
Results may differ from a plain program's by a relative error of at most 0.0003.
Values sent between devices are 32-bit elements; how exact they have to be, the bound alone decides.
No kernel may reach another device: no remote copies, remote signals or barrier semaphores. Data moves between devices by JAX's collectives and lax.ppermute only.
A program may use at most 64 MiB of HBM per device.

v0:
```python
import jax
import jax.numpy as jnp
from jax import lax
from jax.sharding import PartitionSpec as P

STEPS = 4
CYCLES = 3


CENTER = 4.5
RADIUS = 3.5


def passed_along(array, axis, by):
    length = lax.axis_size(axis)
    pairs = [(i, i + by) for i in range(length) if 0 <= i + by < length]
    return lax.ppermute(array, axis, pairs)


def small_solve(matrix, target):
    count = matrix.shape[0]
    lower = [[None] * count for unused in range(count)]
    for outer in range(count):
        for inner in range(outer + 1):
            total = matrix[outer, inner]
            for other in range(inner):
                total = total - lower[outer][other] * lower[inner][other]
            if outer == inner:
                lower[outer][outer] = jnp.sqrt(total)
            else:
                lower[outer][inner] = total / lower[inner][inner]
    solved = []
    for outer in range(count):
        total = target[outer]
        for other in range(outer):
            total = total - lower[outer][other] * solved[other]
        solved.append(total / lower[outer][outer])
    result = [None] * count
    for outer in reversed(range(count)):
        total = solved[outer]
        for other in range(outer + 1, count):
            total = total - lower[other][outer] * result[other]
        result[outer] = total / lower[outer][outer]
    return jnp.stack(result)


def cycle_weights(gram_matrix):
    combined = CENTER * gram_matrix[:-1] + RADIUS * gram_matrix[1:]
    normal_matrix = CENTER * combined[:, :-1] + RADIUS * combined[:, 1:]
    return small_solve(normal_matrix, combined[:, 0])


def residual_weights(weights):
    padding = jnp.zeros((1,) + weights.shape[1:], weights.dtype)
    image = CENTER * jnp.concatenate([weights, padding], 0) + RADIUS * jnp.concatenate(
        [padding, weights], 0
    )
    first = jnp.zeros_like(image).at[0].set(1.0)
    return first - image


def apply_matrix(vector, blocks, block_cols, send_lists):
    block_rows = blocks.shape[0]
    block_size = blocks.shape[2]
    columns = vector.shape[1]
    vector_blocks = vector.reshape(block_rows, block_size, columns)
    to_next = vector_blocks[send_lists[0, 0]]
    to_previous = vector_blocks[send_lists[0, 1]]
    from_previous = passed_along(to_next, "sub", 1)
    from_next = passed_along(to_previous, "sub", -1)
    extended = jnp.concatenate([vector_blocks, from_previous, from_next], 0)
    total = jnp.zeros((block_rows, block_size, columns), jnp.float32)
    for slot in range(blocks.shape[1]):
        total = total + jnp.einsum(
            "bij,bjc->bic",
            blocks[:, slot],
            extended[block_cols[:, slot]],
            precision=lax.Precision.HIGHEST,
        )
    return total.reshape(block_rows * block_size, columns)


def solve_cycles(right_side, blocks, block_cols, send_lists):
    correction = jnp.zeros_like(right_side)
    residual = right_side
    for restart in range(CYCLES):
        krylov = [residual]
        for power in range(STEPS):
            latest = krylov[-1]
            krylov.append(
                (apply_matrix(latest, blocks, block_cols, send_lists) - CENTER * latest) / RADIUS
            )
        stacked = jnp.stack(krylov)
        local_gram = jnp.einsum("irc,jrc->ijc", stacked, stacked, precision=lax.Precision.HIGHEST)
        gram_matrix = lax.psum(local_gram, "sub")
        weights = cycle_weights(gram_matrix)
        combine = residual_weights(weights)
        update = weights[0][None] * krylov[0]
        for power in range(1, STEPS):
            update = update + weights[power][None] * krylov[power]
        correction = correction + update
        fresh = combine[0][None] * krylov[0]
        for power in range(1, STEPS + 1):
            fresh = fresh + combine[power][None] * krylov[power]
        residual = fresh
    return (correction, residual)


def on_device(right_side, blocks, block_cols, send_lists):
    gathered = lax.all_gather(right_side, "fold", axis=0, tiled=True)
    correction, residual = solve_cycles(gathered, blocks, block_cols, send_lists)
    row_count = right_side.shape[0]
    row_start = lax.axis_index("fold") * row_count
    correction = lax.dynamic_slice_in_dim(correction, row_start, row_count, 0)
    residual = lax.dynamic_slice_in_dim(residual, row_start, row_count, 0)
    return (correction, residual)


def solution(mesh):
    placed = (
        P(("sub", "fold"), None),
        P("sub", None, None, None),
        P("sub", None),
        P("sub", None, None),
    )
    return jax.shard_map(
        on_device,
        mesh=mesh,
        in_specs=placed,
        out_specs=(P(("sub", "fold"), None), P(("sub", "fold"), None)),
        check_vma=False,
    )
```

profile of v0, /device:TPU:128, one launch (start us, length us, event | category | flops | bytes accessed | tf_op | source)
XLA Modules:
  0.0 1305.5 jit_solution(807065040131662107)
XLA Ops:
  1.5 7.1 all_gather.3
  9.2 5.4 collective-permute-start.1
  15.2 1.9 collective-permute-start
  19.3 6.3 collective-permute-done
  34.5 1.9 collective-permute-start.2
  37.8 8.1 collective-permute-start.3
  60.0 8.5 collective-permute-start.5
  79.3 1.9 collective-permute-start.6
  82.6 8.6 collective-permute-start.7
  102.5 2.4 stack.74
  105.0 2.2 convolution_bitcast_fusion.2
  107.2 309.9 %psum.21 = f32[5,5,64]{0,1,2:T(8,128)S(1)} all-reduce(f32[5,5,64]{0,1,2:T(8,128)} %convolution_bitcast_fusion.2), channel_id=1, replica_groups=mesh['sub'=64,'fold'=4] {'sub'}, use_global_device_ids=true, to_apply=%region_0.0 | all-reduce | flops 1600 | bytes 12800 | tf_op jit(solution)/shard_map/psum | solution.py:95
  418.9 2.3 slice_reduce_fusion.26
  427.6 8.1 collective-permute-start.9
  449.5 1.9 collective-permute-start.10
  452.0 8.7 collective-permute-start.11
  478.2 8.5 collective-permute-start.13
  503.5 1.9 collective-permute-start.14
  506.0 8.5 collective-permute-start.15
  532.1 4.0 convolution_bitcast_fusion.1
  536.1 309.7 %psum.22 = f32[5,5,64]{0,1,2:T(8,128)S(1)} all-reduce(f32[5,5,64]{0,1,2:T(8,128)S(1)} %convolution_bitcast_fusion.1), channel_id=1, replica_groups=mesh['sub'=64,'fold'=4] {'sub'}, use_global_device_ids=true, to_apply=%region_1.0 | all-reduce | flops 1600 | bytes 12800 | tf_op jit(solution)/shard_map/psum | solution.py:95
  847.7 2.3 slice_reduce_fusion.13
  856.8 1.9 collective-permute-start.16
  859.9 8.1 collective-permute-start.17
  890.8 8.5 collective-permute-start.19
  921.8 2.1 gather_fusion.91
  923.9 8.5 collective-permute-start.21
  955.6 8.4 collective-permute-start.23
  967.5 7.1 collective-permute-done.22
  992.6 4.0 convolution_bitcast_fusion
  996.6 302.8 %psum.23 = f32[5,5,64]{0,1,2:T(8,128)S(1)} all-reduce(f32[5,5,64]{0,1,2:T(8,128)S(1)} %convolution_bitcast_fusion), channel_id=1, replica_groups=mesh['sub'=64,'fold'=4] {'sub'}, use_global_device_ids=true, to_apply=%region_2.0 | all-reduce | flops 1600 | bytes 12800 | tf_op jit(solution)/shard_map/psum | solution.py:95
  1301.2 2.3 slice_reduce_fusion
  (420 shorter events, 228.2 us)
Async XLA Ops:
  9.2 16.4 %collective-permute-start.1 = (f32[2,128,64]{1,2,0:T(8,128)S(1)}, f32[2,128,64]{1,2,0:T(8,128)S(1)}, u32[]{:S(2)}, u32[]{:S(2)}) collective-permute-start(f32[2,128,64]{1,2,0:T(8,128)S(1)} %gather_fusion.1), channel_id=1, source_target_pairs={{4,0},{8,4},{12,8},{16,12},{20,16},{24,20},{28,24},{32,28},{36,32}... | collective-permute-start | bytes 196616 | tf_op jit(solution)/shard_map/ppermute | solution.py:17
  15.2 10.4 collective-permute-start
  34.5 11.4 collective-permute-start.2
  37.8 10.0 collective-permute-start.3
  56.7 11.8 collective-permute-start.4
  60.0 10.4 collective-permute-start.5
  79.3 12.0 collective-permute-start.6
  82.6 10.4 collective-permute-start.7
  105.0 316.5 %copy-start.13 = (f32[5,64]{1,0:T(8,128)S(1)}, f32[5,64]{1,0:T(8,128)}, u32[]{:S(2)}) copy-start(f32[5,64]{1,0:T(8,128)} %constant.103.clone.1) | copy-start | bytes 3844
  424.6 11.2 collective-permute-start.8
  427.6 10.0 collective-permute-start.9
  449.5 11.2 collective-permute-start.10
  452.0 10.4 collective-permute-start.11
  475.7 11.0 collective-permute-start.12
  478.2 10.4 collective-permute-start.13
  503.5 11.0 collective-permute-start.14
  506.0 10.4 collective-permute-start.15
  856.8 11.2 collective-permute-start.16
  859.9 10.0 collective-permute-start.17
  887.6 11.6 collective-permute-start.18
  890.8 10.7 collective-permute-start.19
  919.9 12.6 collective-permute-start.20
  923.9 10.6 collective-permute-start.21
  955.6 19.1 %collective-permute-start.23 = (f32[2,128,64]{1,2,0:T(8,128)}, f32[2,128,64]{1,2,0:T(8,128)S(1)}, u32[]{:S(2)}, u32[]{:S(2)}) collective-permute-start(f32[2,128,64]{1,2,0:T(8,128)} %gather_fusion.100), channel_id=1, source_target_pairs={{4,0},{8,4},{12,8},{16,12},{20,16},{24,20},{28,24},{32,28},{36,32}... | collective-permute-start | bytes 196616 | tf_op jit(solution)/shard_map/ppermute | solution.py:17
  964.0 10.6 collective-permute-start.22
  992.5 312.0 %copy-start.29 = (f32[64]{0:T(128)S(1)}, f32[64]{0:T(128)}, u32[]{:S(2)}) copy-start(f32[64]{0:T(128)} %get-tuple-element.90) | copy-start | bytes 772
  992.5 312.0 %copy-start.30 = (f32[64]{0:T(128)S(1)}, f32[64]{0:T(128)}, u32[]{:S(2)}) copy-start(f32[64]{0:T(128)} %get-tuple-element.94) | copy-start | bytes 772
  992.5 312.0 %copy-start.31 = (f32[64]{0:T(128)S(1)}, f32[64]{0:T(128)}, u32[]{:S(2)}) copy-start(f32[64]{0:T(128)} %broadcast_multiply_fusion.8) | copy-start | bytes 772
  992.5 312.0 %copy-start.32 = (f32[64]{0:T(128)S(1)}, f32[64]{0:T(128)}, u32[]{:S(2)}) copy-start(f32[64]{0:T(128)} %broadcast_multiply_fusion.7) | copy-start | bytes 772
  992.5 312.0 %copy-start.33 = (f32[64]{0:T(128)S(1)}, f32[64]{0:T(128)}, u32[]{:S(2)}) copy-start(f32[64]{0:T(128)} %broadcast_multiply_fusion.6) | copy-start | bytes 772
  992.5 312.0 %copy-start.34 = (f32[64]{0:T(128)S(1)}, f32[64]{0:T(128)}, u32[]{:S(2)}) copy-start(f32[64]{0:T(128)} %broadcast_multiply_fusion.5) | copy-start | bytes 772
  992.6 312.0 %copy-start.35 = (f32[64]{0:T(128)S(1)}, f32[64]{0:T(128)}, u32[]{:S(2)}) copy-start(f32[64]{0:T(128)} %broadcast_multiply_fusion.4) | copy-start | bytes 772
  (29 other events, 1092.1 us)
where the time goes:
time: 1320 us; the launch traced here: 1310 us
  blocking collectives  930 us (70%)
  starting transfers between devices  121 us (9%)
  local copies, waits for them, and re-layouts  117 us (9%)
  matrix products  85.2 us (6%)
  waiting for transfers between devices  29.6 us (2%)
  other arithmetic  20.1 us (2%)
    psum x3, blocking collectives, solve_cycles(): gram_matrix = lax.psum(local_gram, 'sub')  922 us
    ppermute x24, starting transfers between devices, passed_along(): return lax.ppermute(array, axis, pairs)  121 us
    dot_general x84, matrix products, apply_matrix(): jnp.einsum('bij,bjc->bic', blocks[:, slot], extended[block_cols[:, slot]]...  74.9 us
    gather x84, local copies, waits for them, and re-layouts, apply_matrix(): extended[block_cols[:, slot]]  74.7 us
    ppermute x24, waiting for transfers between devices, passed_along(): return lax.ppermute(array, axis, pairs)  29.6 us
  transfers between devices with their start and end apart: 24, of which 12 were waited for; matrix products, arithmetic and copies ran while one was open for 1% of the time, Pallas kernels for 0%

commit v1 on v0

v1 whole, which is shorter than its diff:
```python
import jax
import jax.numpy as jnp
from jax import lax
from jax.experimental import pallas as pl
from jax.experimental.pallas import tpu as pltpu
from jax.sharding import PartitionSpec as P

STEPS = 4
CYCLES = 3
CENTER = 4.5
RADIUS = 3.5
BS = 128
NB = 4
HALO = 2
EXT = NB + 2 * HALO
ROWS = NB * BS
COLS = 32
PAIRS = [(i, j) for i in range(STEPS + 1) for j in range(i, STEPS + 1)]
GROUP = 128 // COLS
GRAM_ROWS = (len(PAIRS) + GROUP - 1) // GROUP

VMEM = pl.BlockSpec(memory_space=pltpu.VMEM)
SMEM = pl.BlockSpec(memory_space=pltpu.SMEM)
PARAMS = pltpu.CompilerParams(vmem_limit_bytes=32 * 1024 * 1024)


def f32(*shape):
    return jax.ShapeDtypeStruct(shape, jnp.float32)


def bf16(*shape):
    return jax.ShapeDtypeStruct(shape, jnp.bfloat16)


def split(value):
    high = value.astype(jnp.bfloat16)
    low = (value - high.astype(jnp.float32)).astype(jnp.bfloat16)
    return high, low


def write_sends(lists, vector, to_next, to_previous):
    for slot in range(HALO):
        for side, target in ((0, to_next), (1, to_previous)):
            start = pl.multiple_of(lists[side, slot] * BS, BS)
            target[:, slot * BS : (slot + 1) * BS] = vector[:, pl.ds(start, BS)]


def operator_kernel(cols, blocks, high, low, dense):
    dense[...] = jnp.zeros_like(dense)
    for row in range(NB):
        for slot in range(blocks.shape[1]):
            start = pl.multiple_of(cols[row, slot] * BS, BS)
            place = (pl.ds(start, BS), slice(row * BS, (row + 1) * BS))
            dense[place] = dense[place] + blocks[row, slot].T
    unit = (
        lax.broadcasted_iota(jnp.int32, (BS, BS), 0) == lax.broadcasted_iota(jnp.int32, (BS, BS), 1)
    ).astype(jnp.float32)
    for row in range(NB):
        for column in range(EXT):
            place = (slice(column * BS, (column + 1) * BS), slice(row * BS, (row + 1) * BS))
            value = dense[place]
            if row == column:
                value = value - CENTER * unit
            high[place], low[place] = split(value * (1.0 / RADIUS))


def start_kernel(lists, core, gathered, vector, to_next, to_previous):
    first = pl.multiple_of(core[0] * COLS, COLS)
    vector[...] = gathered[pl.ds(first, COLS), :]
    write_sends(lists, vector, to_next, to_previous)


def step_kernel(lists, vector, from_previous, from_next, high, low, result, to_next, to_previous):
    extended = jnp.concatenate([vector[...], from_previous[...], from_next[...]], 1)
    top, rest = split(extended)
    first = jnp.dot(
        jnp.concatenate([top, rest], 0), high[...], preferred_element_type=jnp.float32
    )
    second = jnp.dot(top, low[...], preferred_element_type=jnp.float32)
    result[...] = first[:COLS] + (first[COLS:] + second)
    write_sends(lists, result, to_next, to_previous)


def local_gram(vectors, gram):
    products = []
    for i, j in PAIRS:
        total = None
        for tile in range(NB):
            place = slice(tile * BS, (tile + 1) * BS)
            term = vectors[i][:, place] * vectors[j][:, place]
            total = term if total is None else total + term
        products.append(total)
    while len(products) < GRAM_ROWS * GROUP:
        products.append(jnp.zeros((COLS, BS), jnp.float32))
    sums = lax.dot_general(
        jnp.ones((8, BS), jnp.float32),
        jnp.concatenate(products, 0),
        (((1,), (1,)), ((), ())),
        precision=lax.Precision.HIGHEST,
        preferred_element_type=jnp.float32,
    )
    packed = jnp.concatenate([sums[:1, row * BS : (row + 1) * BS] for row in range(GRAM_ROWS)], 0)
    gram[...] = jnp.broadcast_to(packed[None], gram.shape)


def gram_kernel(*refs):
    local_gram([ref[...] for ref in refs[:-1]], refs[-1])


def small_solve(matrix, target):
    count = len(target)
    lower = [[None] * count for unused in range(count)]
    inverse = [None] * count
    for outer in range(count):
        for inner in range(outer + 1):
            total = matrix[outer][inner]
            for other in range(inner):
                total = total - lower[outer][other] * lower[inner][other]
            if outer == inner:
                inverse[outer] = 1.0 / jnp.sqrt(total)
            else:
                lower[outer][inner] = total * inverse[inner]
    solved = []
    for outer in range(count):
        total = target[outer]
        for other in range(outer):
            total = total - lower[outer][other] * solved[other]
        solved.append(total * inverse[outer])
    result = [None] * count
    for outer in reversed(range(count)):
        total = solved[outer]
        for other in range(outer + 1, count):
            total = total - lower[other][outer] * result[other]
        result[outer] = total * inverse[outer]
    return result


def cycle_weights(gathered):
    summed = jnp.sum(gathered, 0)
    padded = jnp.concatenate([summed, jnp.zeros((8 - GRAM_ROWS, BS), jnp.float32)], 0)
    turned = padded.T
    gram = [[None] * (STEPS + 1) for unused in range(STEPS + 1)]
    for index, (i, j) in enumerate(PAIRS):
        first = (index % GROUP) * COLS
        column = turned[first : first + COLS, index // GROUP : index // GROUP + 1]
        gram[i][j] = gram[j][i] = jnp.broadcast_to(column, (COLS, BS))
    combined = [
        [CENTER * gram[i][j] + RADIUS * gram[i + 1][j] for j in range(STEPS + 1)]
        for i in range(STEPS)
    ]
    normal = [
        [CENTER * combined[i][j] + RADIUS * combined[i][j + 1] for j in range(STEPS)]
        for i in range(STEPS)
    ]
    weights = small_solve(normal, [combined[i][0] for i in range(STEPS)])
    left = [1.0 - CENTER * weights[0]]
    for i in range(1, STEPS):
        left.append(-(CENTER * weights[i] + RADIUS * weights[i - 1]))
    left.append(-(RADIUS * weights[STEPS - 1]))
    return weights, left


def combined_tile(weights, vectors, tile):
    place = slice(tile * BS, (tile + 1) * BS)
    total = None
    for weight, vector in zip(weights, vectors):
        term = weight * vector[:, place]
        total = term if total is None else total + term
    return total


def restart_kernel(has_correction, *refs):
    lists, gathered = refs[:2]
    vectors = refs[2 : 2 + 2 * STEPS + 1]
    refs = refs[2 + 2 * STEPS + 1 :]
    if has_correction:
        old, refs = refs[0], refs[1:]
    correction, fresh, gram, to_next, to_previous = refs[0], refs[1:-3], *refs[-3:]
    weights, left = cycle_weights(gathered[...])
    for tile in range(NB):
        place = slice(tile * BS, (tile + 1) * BS)
        update = combined_tile(weights, vectors, tile)
        correction[:, place] = old[:, place] + update if has_correction else update
        for power in range(STEPS + 1):
            fresh[power][:, place] = combined_tile(left, vectors[power:], tile)
    write_sends(lists, fresh[STEPS], to_next, to_previous)
    local_gram([ref[...] for ref in fresh], gram)


def finish_kernel(gathered, *refs):
    vectors = refs[: STEPS + 1]
    old, correction, residual = refs[STEPS + 1 :]
    weights, left = cycle_weights(gathered[...])
    for tile in range(NB):
        place = slice(tile * BS, (tile + 1) * BS)
        correction[:, place] = old[:, place] + combined_tile(weights, vectors, tile)
        residual[:, place] = combined_tile(left, vectors, tile)


def call(kernel, out_shape, smem, vmem, scratch=()):
    return pl.pallas_call(
        kernel,
        out_shape=out_shape,
        in_specs=[SMEM] * len(smem) + [VMEM] * len(vmem),
        out_specs=jax.tree.map(lambda unused: VMEM, out_shape),
        scratch_shapes=scratch,
        compiler_params=PARAMS,
    )(*smem, *vmem)


def on_device(right_side, blocks, block_cols, send_lists):
    subs = lax.axis_size("sub")
    lists = send_lists[0]
    fold = lax.axis_index("fold")
    core = fold % 2
    vector_shape = f32(COLS, ROWS)
    halo_shape = f32(COLS, HALO * BS)
    gram_shape = f32(subs, GRAM_ROWS, BS)
    high, low = call(
        operator_kernel,
        (bf16(EXT * BS, ROWS), bf16(EXT * BS, ROWS)),
        [block_cols],
        [blocks],
        [pltpu.VMEM((EXT * BS, ROWS), jnp.float32)],
    )
    gathered = lax.all_gather(right_side.T, "fold", axis=1, tiled=True)
    vector, to_next, to_previous = call(
        start_kernel,
        (vector_shape, halo_shape, halo_shape),
        [lists, core.astype(jnp.int32).reshape(1)],
        [gathered],
    )

    def passed(value, by):
        return lax.ppermute(value, "sub", [(i, (i + by) % subs) for i in range(subs)])

    def step(vector, to_next, to_previous):
        from_previous = passed(to_next, 1)
        from_next = passed(to_previous, -1)
        return call(
            step_kernel,
            (vector_shape, halo_shape, halo_shape),
            [lists],
            [vector, from_previous, from_next, high, low],
        )

    def exchanged(gram):
        return lax.all_to_all(gram, "sub", 0, 0)

    basis = [vector]
    for power in range(STEPS):
        vector, to_next, to_previous = step(vector, to_next, to_previous)
        basis.append(vector)
    gram = call(gram_kernel, gram_shape, [], basis)
    correction = None
    for restart in range(CYCLES - 1):
        sums = exchanged(gram)
        for power in range(STEPS):
            vector, to_next, to_previous = step(vector, to_next, to_previous)
            basis.append(vector)
        old = [] if correction is None else [correction]
        results = call(
            lambda *refs, held=bool(old): restart_kernel(held, *refs),
            (vector_shape,) * (STEPS + 2) + (gram_shape, halo_shape, halo_shape),
            [lists],
            [sums, *basis, *old],
        )
        correction, basis = results[0], list(results[1 : STEPS + 2])
        gram, to_next, to_previous = results[-3:]
        vector = basis[-1]
    correction, residual = call(
        finish_kernel,
        (vector_shape, vector_shape),
        [],
        [exchanged(gram), *basis, correction],
    )
    both = jnp.stack([correction, residual])
    other = lax.dynamic_slice_in_dim(both, (fold - core + 1 - core) * BS, BS, 2)
    arrived = lax.ppermute(other, "fold", [(0, 1), (1, 0), (2, 3), (3, 2)])
    own = lax.dynamic_slice_in_dim(both, fold * BS, BS, 2)
    whole = jnp.where(
        core == 0, jnp.concatenate([own, arrived], 1), jnp.concatenate([arrived, own], 1)
    )
    return (whole[0].T, whole[1].T)


def solution(mesh):
    placed = (
        P(("sub", "fold"), None),
        P("sub", None, None, None),
        P("sub", None),
        P("sub", None, None),
    )
    return jax.shard_map(
        on_device,
        mesh=mesh,
        in_specs=placed,
        out_specs=(P(("sub", "fold"), None), P(("sub", "fold"), None)),
        check_vma=False,
    )
```

time: 1320 us -> 181 us (0.14)
  the two profiles are of different devices: /device:TPU:128 before, /device:TPU:1 now
where the time goes in v1:
time: 181 us; the launch traced here: 180 us
  starting transfers between devices  119 us (66%)
  waiting for transfers between devices  24.7 us (14%)
  Pallas kernels  21.7 us (12%)
  blocking collectives  10.2 us (6%)
  local copies, waits for them, and re-layouts  3.5 us (2%)
    ppermute x24, starting transfers between devices, passed(): lax.ppermute(value, 'sub', [(i, (i + by) % subs) for i in range(subs)])  72.8 us
    all_to_all x3, starting transfers between devices, exchanged(): return lax.all_to_all(gram, 'sub', 0, 0)  30.9 us
    pallas_call x18, Pallas kernels, call(): pl.pallas_call(kernel, out_shape=out_shape, in_specs=[SMEM] * len(smem) +...  21.7 us
    ppermute x1, starting transfers between devices, on_device(): arrived = lax.ppermute(other, 'fold', [(0, 1), (1, 0), (2, 3), (3, 2)])  15.6 us
    ppermute x24, waiting for transfers between devices, passed(): lax.ppermute(value, 'sub', [(i, (i + by) % subs) for i in range(subs)])  14.1 us
    all_gather x1, blocking collectives, on_device(): gathered = lax.all_gather(right_side.T, 'fold', axis=1, tiled=True)  10.2 us
    all_to_all x3, waiting for transfers between devices, exchanged(): return lax.all_to_all(gram, 'sub', 0, 0)  9.8 us
  transfers between devices with their start and end apart: 28, of which 13 were waited for; matrix products, arithmetic and copies ran while one was open for 0% of the time, Pallas kernels for 6%

profile of v1, /device:TPU:1, one launch (start us, length us, event | category | flops | bytes accessed | tf_op | source)
XLA Modules:
  0.0 180.4 jit_solution(15062261957759250527)
XLA Ops:
  0.6 10.2 %all_gather.3.gathered = f32[64,512]{1,0:T(8,128)S(1)} all-gather(f32[64,128]{1,0:T(8,128)} %bitcast.30), channel_id=1, replica_groups=mesh['sub'=64,'fold'=4] {'fold'}, dimensions={1}, use_global_device_ids=true | all-gather | bytes 163840 | tf_op jit(solution)/shard_map/all_gather | solution.py:226
  12.2 7.3 %collective-permute-start.1 = (f32[32,256]{1,0:T(8,128)S(1)}, f32[32,256]{1,0:T(8,128)S(1)}, u32[]{:S(2)}, u32[]{:S(2)}) collective-permute-start(f32[32,256]{1,0:T(8,128)S(1)} %get-tuple-element.59), channel_id=1, source_target_pairs={{0,252},{4,0},{8,4},{12,8},{16,12},{20,16},{24,20},{28,24},{32,28}... | collective-permute-start | bytes 98312 | tf_op jit(solution)/shard_map/ppermute | solution.py:235
  19.5 1.5 copy-done
  21.7 1.7 shard_map.60
  24.6 5.7 %collective-permute-start.3 = (f32[32,256]{1,0:T(8,128)S(1)}, f32[32,256]{1,0:T(8,128)S(1)}, u32[]{:S(2)}, u32[]{:S(2)}) collective-permute-start(f32[32,256]{1,0:T(8,128)S(1)} %get-tuple-element.64), channel_id=1, source_target_pairs={{0,252},{4,0},{8,4},{12,8},{16,12},{20,16},{24,20},{28,24},{32,28}... | collective-permute-start | bytes 98312 | tf_op jit(solution)/shard_map/ppermute | solution.py:235
  30.2 1.3 collective-permute-done.2.from_previous
  32.7 5.9 %collective-permute-start.5 = (f32[32,256]{1,0:T(8,128)S(1)}, f32[32,256]{1,0:T(8,128)S(1)}, u32[]{:S(2)}, u32[]{:S(2)}) collective-permute-start(f32[32,256]{1,0:T(8,128)S(1)} %get-tuple-element.67), channel_id=1, source_target_pairs={{0,252},{4,0},{8,4},{12,8},{16,12},{20,16},{24,20},{28,24},{32,28}... | collective-permute-start | bytes 98312 | tf_op jit(solution)/shard_map/ppermute | solution.py:235
  38.5 1.2 collective-permute-done.4.from_previous
  40.9 5.8 %collective-permute-start.7 = (f32[32,256]{1,0:T(8,128)S(1)}, f32[32,256]{1,0:T(8,128)S(1)}, u32[]{:S(2)}, u32[]{:S(2)}) collective-permute-start(f32[32,256]{1,0:T(8,128)S(1)} %get-tuple-element.70), channel_id=1, source_target_pairs={{0,252},{4,0},{8,4},{12,8},{16,12},{20,16},{24,20},{28,24},{32,28}... | collective-permute-start | bytes 98312 | tf_op jit(solution)/shard_map/ppermute | solution.py:235
  46.7 1.2 collective-permute-done.6.from_previous
  50.1 9.1 %all-to-all-start = ((f32[64,4,128]{2,1,0:T(4,128)}), f32[64,4,128]{2,1,0:T(4,128)S(1)}, u32[]{:S(2)}, u32[]{:S(2)}) async-start(f32[64,4,128]{2,1,0:T(4,128)} %shard_map.65), calls=%async_computation | async-start | bytes 262144 | tf_op jit(solution)/shard_map/all_to_all | solution.py:248
  60.3 4.7 %collective-permute-start.9 = (f32[32,256]{1,0:T(8,128)S(1)}, f32[32,256]{1,0:T(8,128)S(1)}, u32[]{:S(2)}, u32[]{:S(2)}) collective-permute-start(f32[32,256]{1,0:T(8,128)S(1)} %get-tuple-element.73), channel_id=1, source_target_pairs={{0,252},{4,0},{8,4},{12,8},{16,12},{20,16},{24,20},{28,24},{32,28}... | collective-permute-start | bytes 98312 | tf_op jit(solution)/shard_map/ppermute | solution.py:235
  65.0 1.5 collective-permute-done.8.from_previous
  67.8 6.4 %collective-permute-start.11 = (f32[32,256]{1,0:T(8,128)S(1)}, f32[32,256]{1,0:T(8,128)S(1)}, u32[]{:S(2)}, u32[]{:S(2)}) collective-permute-start(f32[32,256]{1,0:T(8,128)S(1)} %get-tuple-element.76), channel_id=1, source_target_pairs={{0,252},{4,0},{8,4},{12,8},{16,12},{20,16},{24,20},{28,24},{32,28}... | collective-permute-start | bytes 98312 | tf_op jit(solution)/shard_map/ppermute | solution.py:235
  74.2 1.2 collective-permute-done.10.from_previous
  76.5 5.9 %collective-permute-start.13 = (f32[32,256]{1,0:T(8,128)S(1)}, f32[32,256]{1,0:T(8,128)S(1)}, u32[]{:S(2)}, u32[]{:S(2)}) collective-permute-start(f32[32,256]{1,0:T(8,128)S(1)} %get-tuple-element.79), channel_id=1, source_target_pairs={{0,252},{4,0},{8,4},{12,8},{16,12},{20,16},{24,20},{28,24},{32,28}... | collective-permute-start | bytes 98312 | tf_op jit(solution)/shard_map/ppermute | solution.py:235
  84.8 5.8 %collective-permute-start.15 = (f32[32,256]{1,0:T(8,128)S(1)}, f32[32,256]{1,0:T(8,128)S(1)}, u32[]{:S(2)}, u32[]{:S(2)}) collective-permute-start(f32[32,256]{1,0:T(8,128)S(1)} %get-tuple-element.82), channel_id=1, source_target_pairs={{0,252},{4,0},{8,4},{12,8},{16,12},{20,16},{24,20},{28,24},{32,28}... | collective-permute-start | bytes 98312 | tf_op jit(solution)/shard_map/ppermute | solution.py:235
  91.8 1.7 shard_map.69
  93.5 2.2 %shard_map.70 = (f32[32,512]{1,0:T(8,128)S(1)}, f32[32,512]{1,0:T(8,128)S(1)}, f32[32,512]{1,0:T(8,128)S(1)}, f32[32,512]{1,0:T(8,128)S(1)}, f32[32,512]{1,0:T(8...) custom-call(s32[2,2]{1,0:T(2,128)S(1)} %bitcast.22, ...), custom_call_target="tpu_custom_call" | custom-call | tf_op jit(solution)/shard_map/pallas_call | solution.py:201
  95.7 10.7 %all-to-all-start.1 = ((f32[64,4,128]{2,1,0:T(4,128)}), f32[64,4,128]{2,1,0:T(4,128)S(1)}, u32[]{:S(2)}, u32[]{:S(2)}) async-start(f32[64,4,128]{2,1,0:T(4,128)} %get-tuple-element.84), calls=%async_computation.1 | async-start | bytes 262144 | tf_op jit(solution)/shard_map/all_to_all | solution.py:248
  107.5 4.7 %collective-permute-start.17 = (f32[32,256]{1,0:T(8,128)S(1)}, f32[32,256]{1,0:T(8,128)S(1)}, u32[]{:S(2)}, u32[]{:S(2)}) collective-permute-start(f32[32,256]{1,0:T(8,128)S(1)} %get-tuple-element.91), channel_id=1, source_target_pairs={{0,252},{4,0},{8,4},{12,8},{16,12},{20,16},{24,20},{28,24},{32,28}... | collective-permute-start | bytes 98312 | tf_op jit(solution)/shard_map/ppermute | solution.py:235
  112.2 1.5 collective-permute-done.16.from_previous
  114.8 5.7 %collective-permute-start.19 = (f32[32,256]{1,0:T(8,128)S(1)}, f32[32,256]{1,0:T(8,128)S(1)}, u32[]{:S(2)}, u32[]{:S(2)}) collective-permute-start(f32[32,256]{1,0:T(8,128)S(1)} %get-tuple-element.94), channel_id=1, source_target_pairs={{0,252},{4,0},{8,4},{12,8},{16,12},{20,16},{24,20},{28,24},{32,28}... | collective-permute-start | bytes 98312 | tf_op jit(solution)/shard_map/ppermute | solution.py:235
  120.5 1.4 collective-permute-done.18.from_previous
  123.0 5.7 %collective-permute-start.21 = (f32[32,256]{1,0:T(8,128)S(1)}, f32[32,256]{1,0:T(8,128)S(1)}, u32[]{:S(2)}, u32[]{:S(2)}) collective-permute-start(f32[32,256]{1,0:T(8,128)S(1)} %get-tuple-element.97), channel_id=1, source_target_pairs={{0,252},{4,0},{8,4},{12,8},{16,12},{20,16},{24,20},{28,24},{32,28}... | collective-permute-start | bytes 98312 | tf_op jit(solution)/shard_map/ppermute | solution.py:235
  128.7 1.3 collective-permute-done.20.from_previous
  131.0 6.0 %collective-permute-start.23 = (f32[32,256]{1,0:T(8,128)S(1)}, f32[32,256]{1,0:T(8,128)S(1)}, u32[]{:S(2)}, u32[]{:S(2)}) collective-permute-start(f32[32,256]{1,0:T(8,128)S(1)} %get-tuple-element.100), channel_id=1, source_target_pairs={{0,252},{4,0},{8,4},{12,8},{16,12},{20,16},{24,20},{28,24},{32,28}... | collective-permute-start | bytes 98312 | tf_op jit(solution)/shard_map/ppermute | solution.py:235
  138.1 1.6 shard_map.74
  139.8 2.2 %shard_map.75 = (f32[32,512]{1,0:T(8,128)S(1)}, f32[32,512]{1,0:T(8,128)S(1)}, f32[32,512]{1,0:T(8,128)S(1)}, f32[32,512]{1,0:T(8,128)S(1)}, f32[32,512]{1,0:T(8...) custom-call(s32[2,2]{1,0:T(2,128)S(1)} %bitcast.27, ...), custom_call_target="tpu_custom_call" | custom-call | tf_op jit(solution)/shard_map/pallas_call | solution.py:201
  141.9 11.1 %all-to-all-start.2 = ((f32[64,4,128]{2,1,0:T(4,128)}), f32[64,4,128]{2,1,0:T(4,128)S(1)}, u32[]{:S(2)}, u32[]{:S(2)}) async-start(f32[64,4,128]{2,1,0:T(4,128)} %get-tuple-element.103), calls=%async_computation.2 | async-start | bytes 262144 | tf_op jit(solution)/shard_map/all_to_all | solution.py:248
  153.0 9.8 %all-to-all-done.2.gathered = f32[64,4,128]{2,1,0:T(4,128)S(1)} async-done(((f32[64,4,128]{2,1,0:T(4,128)}), f32[64,4,128]{2,1,0:T(4,128)S(1)}, u32[]{:S(2)}, u32[]{:S(2)}) %all-to-all-start.2) | async-done | bytes 131104 | tf_op jit(solution)/shard_map/all_to_all | solution.py:248
  163.2 15.6 %collective-permute-start.24 = (f32[2,32,128]{2,1,0:T(8,128)S(1)}, f32[2,32,128]{2,1,0:T(8,128)S(1)}, u32[]{:S(2)}, u32[]{:S(2)}) collective-permute-start(f32[2,32,128]{2,1,0:T(8,128)S(1)} %get-tuple-element.113), channel_id=1, source_target_pairs={{0,1},{1,0},{2,3},{3,2},{4,5},{5,4},{6,7},{7,6},{8,9},{9,8},{10,11... | collective-permute-start | bytes 98312 | tf_op jit(solution)/shard_map/ppermute | solution.py:279
  (54 shorter events, 21.9 us)
Async XLA Ops:
  0.6 22.8 %copy-start.2 = (s32[1,2,2]{2,1,0:T(2,128)S(1)}, s32[1,2,2]{2,1,0:T(2,128)}, u32[]{:S(2)}) copy-start(s32[1,2,2]{2,1,0:T(2,128)} %param.7) | copy-start | bytes 52
  10.9 0.7 copy-start.1
  12.1 11.3 %collective-permute-start = (f32[32,256]{1,0:T(8,128)S(1)}, f32[32,256]{1,0:T(8,128)S(1)}, u32[]{:S(2)}, u32[]{:S(2)}) collective-permute-start(f32[32,256]{1,0:T(8,128)S(1)} %get-tuple-element.58), channel_id=1, source_target_pairs={{0,4},{4,8},{8,12},{12,16},{16,20},{20,24},{24,28},{28,32},{32,36}... | collective-permute-start | bytes 98312 | tf_op jit(solution)/shard_map/ppermute | solution.py:235
  12.2 11.2 %collective-permute-start.1 = (f32[32,256]{1,0:T(8,128)S(1)}, f32[32,256]{1,0:T(8,128)S(1)}, u32[]{:S(2)}, u32[]{:S(2)}) collective-permute-start(f32[32,256]{1,0:T(8,128)S(1)} %get-tuple-element.59), channel_id=1, source_target_pairs={{0,252},{4,0},{8,4},{12,8},{16,12},{20,16},{24,20},{28,24},{32,28}... | collective-permute-start | bytes 98312 | tf_op jit(solution)/shard_map/ppermute | solution.py:235
  19.5 1.5 copy-start
  21.0 0.7 copy-start.3
  24.5 7.1 %collective-permute-start.2 = (f32[32,256]{1,0:T(8,128)S(1)}, f32[32,256]{1,0:T(8,128)S(1)}, u32[]{:S(2)}, u32[]{:S(2)}) collective-permute-start(f32[32,256]{1,0:T(8,128)S(1)} %get-tuple-element.63), channel_id=1, source_target_pairs={{0,4},{4,8},{8,12},{12,16},{16,20},{20,24},{24,28},{28,32},{32,36}... | collective-permute-start | bytes 98312 | tf_op jit(solution)/shard_map/ppermute | solution.py:235
  24.6 7.0 %collective-permute-start.3 = (f32[32,256]{1,0:T(8,128)S(1)}, f32[32,256]{1,0:T(8,128)S(1)}, u32[]{:S(2)}, u32[]{:S(2)}) collective-permute-start(f32[32,256]{1,0:T(8,128)S(1)} %get-tuple-element.64), channel_id=1, source_target_pairs={{0,252},{4,0},{8,4},{12,8},{16,12},{20,16},{24,20},{28,24},{32,28}... | collective-permute-start | bytes 98312 | tf_op jit(solution)/shard_map/ppermute | solution.py:235
  32.6 7.2 %collective-permute-start.4 = (f32[32,256]{1,0:T(8,128)S(1)}, f32[32,256]{1,0:T(8,128)S(1)}, u32[]{:S(2)}, u32[]{:S(2)}) collective-permute-start(f32[32,256]{1,0:T(8,128)S(1)} %get-tuple-element.66), channel_id=1, source_target_pairs={{0,4},{4,8},{8,12},{12,16},{16,20},{20,24},{24,28},{28,32},{32,36}... | collective-permute-start | bytes 98312 | tf_op jit(solution)/shard_map/ppermute | solution.py:235
  32.7 7.1 %collective-permute-start.5 = (f32[32,256]{1,0:T(8,128)S(1)}, f32[32,256]{1,0:T(8,128)S(1)}, u32[]{:S(2)}, u32[]{:S(2)}) collective-permute-start(f32[32,256]{1,0:T(8,128)S(1)} %get-tuple-element.67), channel_id=1, source_target_pairs={{0,252},{4,0},{8,4},{12,8},{16,12},{20,16},{24,20},{28,24},{32,28}... | collective-permute-start | bytes 98312 | tf_op jit(solution)/shard_map/ppermute | solution.py:235
  40.8 7.1 %collective-permute-start.6 = (f32[32,256]{1,0:T(8,128)S(1)}, f32[32,256]{1,0:T(8,128)S(1)}, u32[]{:S(2)}, u32[]{:S(2)}) collective-permute-start(f32[32,256]{1,0:T(8,128)S(1)} %get-tuple-element.69), channel_id=1, source_target_pairs={{0,4},{4,8},{8,12},{12,16},{16,20},{20,24},{24,28},{28,32},{32,36}... | collective-permute-start | bytes 98312 | tf_op jit(solution)/shard_map/ppermute | solution.py:235
  40.9 7.1 %collective-permute-start.7 = (f32[32,256]{1,0:T(8,128)S(1)}, f32[32,256]{1,0:T(8,128)S(1)}, u32[]{:S(2)}, u32[]{:S(2)}) collective-permute-start(f32[32,256]{1,0:T(8,128)S(1)} %get-tuple-element.70), channel_id=1, source_target_pairs={{0,252},{4,0},{8,4},{12,8},{16,12},{20,16},{24,20},{28,24},{32,28}... | collective-permute-start | bytes 98312 | tf_op jit(solution)/shard_map/ppermute | solution.py:235
  50.1 43.4 %all-to-all-start = ((f32[64,4,128]{2,1,0:T(4,128)}), f32[64,4,128]{2,1,0:T(4,128)S(1)}, u32[]{:S(2)}, u32[]{:S(2)}) async-start(f32[64,4,128]{2,1,0:T(4,128)} %shard_map.65), calls=%async_computation | async-start | bytes 262144 | tf_op jit(solution)/shard_map/all_to_all | solution.py:248
  59.2 7.3 %collective-permute-start.8 = (f32[32,256]{1,0:T(8,128)S(1)}, f32[32,256]{1,0:T(8,128)S(1)}, u32[]{:S(2)}, u32[]{:S(2)}) collective-permute-start(f32[32,256]{1,0:T(8,128)S(1)} %get-tuple-element.72), channel_id=1, source_target_pairs={{0,4},{4,8},{8,12},{12,16},{16,20},{20,24},{24,28},{28,32},{32,36}... | collective-permute-start | bytes 98312 | tf_op jit(solution)/shard_map/ppermute | solution.py:235
  60.3 6.2 %collective-permute-start.9 = (f32[32,256]{1,0:T(8,128)S(1)}, f32[32,256]{1,0:T(8,128)S(1)}, u32[]{:S(2)}, u32[]{:S(2)}) collective-permute-start(f32[32,256]{1,0:T(8,128)S(1)} %get-tuple-element.73), channel_id=1, source_target_pairs={{0,252},{4,0},{8,4},{12,8},{16,12},{20,16},{24,20},{28,24},{32,28}... | collective-permute-start | bytes 98312 | tf_op jit(solution)/shard_map/ppermute | solution.py:235
  67.5 7.8 %collective-permute-start.10 = (f32[32,256]{1,0:T(8,128)S(1)}, f32[32,256]{1,0:T(8,128)S(1)}, u32[]{:S(2)}, u32[]{:S(2)}) collective-permute-start(f32[32,256]{1,0:T(8,128)S(1)} %get-tuple-element.75), channel_id=1, source_target_pairs={{0,4},{4,8},{8,12},{12,16},{16,20},{20,24},{24,28},{28,32},{32,36}... | collective-permute-start | bytes 98312 | tf_op jit(solution)/shard_map/ppermute | solution.py:235
  67.8 7.6 %collective-permute-start.11 = (f32[32,256]{1,0:T(8,128)S(1)}, f32[32,256]{1,0:T(8,128)S(1)}, u32[]{:S(2)}, u32[]{:S(2)}) collective-permute-start(f32[32,256]{1,0:T(8,128)S(1)} %get-tuple-element.76), channel_id=1, source_target_pairs={{0,252},{4,0},{8,4},{12,8},{16,12},{20,16},{24,20},{28,24},{32,28}... | collective-permute-start | bytes 98312 | tf_op jit(solution)/shard_map/ppermute | solution.py:235
  76.4 7.3 %collective-permute-start.12 = (f32[32,256]{1,0:T(8,128)S(1)}, f32[32,256]{1,0:T(8,128)S(1)}, u32[]{:S(2)}, u32[]{:S(2)}) collective-permute-start(f32[32,256]{1,0:T(8,128)S(1)} %get-tuple-element.78), channel_id=1, source_target_pairs={{0,4},{4,8},{8,12},{12,16},{16,20},{20,24},{24,28},{28,32},{32,36}... | collective-permute-start | bytes 98312 | tf_op jit(solution)/shard_map/ppermute | solution.py:235
  76.5 7.2 %collective-permute-start.13 = (f32[32,256]{1,0:T(8,128)S(1)}, f32[32,256]{1,0:T(8,128)S(1)}, u32[]{:S(2)}, u32[]{:S(2)}) collective-permute-start(f32[32,256]{1,0:T(8,128)S(1)} %get-tuple-element.79), channel_id=1, source_target_pairs={{0,252},{4,0},{8,4},{12,8},{16,12},{20,16},{24,20},{28,24},{32,28}... | collective-permute-start | bytes 98312 | tf_op jit(solution)/shard_map/ppermute | solution.py:235
  84.7 7.1 %collective-permute-start.14 = (f32[32,256]{1,0:T(8,128)S(1)}, f32[32,256]{1,0:T(8,128)S(1)}, u32[]{:S(2)}, u32[]{:S(2)}) collective-permute-start(f32[32,256]{1,0:T(8,128)S(1)} %get-tuple-element.81), channel_id=1, source_target_pairs={{0,4},{4,8},{8,12},{12,16},{16,20},{20,24},{24,28},{28,32},{32,36}... | collective-permute-start | bytes 98312 | tf_op jit(solution)/shard_map/ppermute | solution.py:235
  84.8 7.1 %collective-permute-start.15 = (f32[32,256]{1,0:T(8,128)S(1)}, f32[32,256]{1,0:T(8,128)S(1)}, u32[]{:S(2)}, u32[]{:S(2)}) collective-permute-start(f32[32,256]{1,0:T(8,128)S(1)} %get-tuple-element.82), channel_id=1, source_target_pairs={{0,252},{4,0},{8,4},{12,8},{16,12},{20,16},{24,20},{28,24},{32,28}... | collective-permute-start | bytes 98312 | tf_op jit(solution)/shard_map/ppermute | solution.py:235
  95.7 44.1 %all-to-all-start.1 = ((f32[64,4,128]{2,1,0:T(4,128)}), f32[64,4,128]{2,1,0:T(4,128)S(1)}, u32[]{:S(2)}, u32[]{:S(2)}) async-start(f32[64,4,128]{2,1,0:T(4,128)} %get-tuple-element.84), calls=%async_computation.1 | async-start | bytes 262144 | tf_op jit(solution)/shard_map/all_to_all | solution.py:248
  106.4 7.3 %collective-permute-start.16 = (f32[32,256]{1,0:T(8,128)S(1)}, f32[32,256]{1,0:T(8,128)S(1)}, u32[]{:S(2)}, u32[]{:S(2)}) collective-permute-start(f32[32,256]{1,0:T(8,128)S(1)} %get-tuple-element.90), channel_id=1, source_target_pairs={{0,4},{4,8},{8,12},{12,16},{16,20},{20,24},{24,28},{28,32},{32,36}... | collective-permute-start | bytes 98312 | tf_op jit(solution)/shard_map/ppermute | solution.py:235
  107.5 6.2 %collective-permute-start.17 = (f32[32,256]{1,0:T(8,128)S(1)}, f32[32,256]{1,0:T(8,128)S(1)}, u32[]{:S(2)}, u32[]{:S(2)}) collective-permute-start(f32[32,256]{1,0:T(8,128)S(1)} %get-tuple-element.91), channel_id=1, source_target_pairs={{0,252},{4,0},{8,4},{12,8},{16,12},{20,16},{24,20},{28,24},{32,28}... | collective-permute-start | bytes 98312 | tf_op jit(solution)/shard_map/ppermute | solution.py:235
  114.7 7.1 %collective-permute-start.18 = (f32[32,256]{1,0:T(8,128)S(1)}, f32[32,256]{1,0:T(8,128)S(1)}, u32[]{:S(2)}, u32[]{:S(2)}) collective-permute-start(f32[32,256]{1,0:T(8,128)S(1)} %get-tuple-element.93), channel_id=1, source_target_pairs={{0,4},{4,8},{8,12},{12,16},{16,20},{20,24},{24,28},{28,32},{32,36}... | collective-permute-start | bytes 98312 | tf_op jit(solution)/shard_map/ppermute | solution.py:235
  114.8 7.0 %collective-permute-start.19 = (f32[32,256]{1,0:T(8,128)S(1)}, f32[32,256]{1,0:T(8,128)S(1)}, u32[]{:S(2)}, u32[]{:S(2)}) collective-permute-start(f32[32,256]{1,0:T(8,128)S(1)} %get-tuple-element.94), channel_id=1, source_target_pairs={{0,252},{4,0},{8,4},{12,8},{16,12},{20,16},{24,20},{28,24},{32,28}... | collective-permute-start | bytes 98312 | tf_op jit(solution)/shard_map/ppermute | solution.py:235
  122.9 7.1 %collective-permute-start.20 = (f32[32,256]{1,0:T(8,128)S(1)}, f32[32,256]{1,0:T(8,128)S(1)}, u32[]{:S(2)}, u32[]{:S(2)}) collective-permute-start(f32[32,256]{1,0:T(8,128)S(1)} %get-tuple-element.96), channel_id=1, source_target_pairs={{0,4},{4,8},{8,12},{12,16},{16,20},{20,24},{24,28},{28,32},{32,36}... | collective-permute-start | bytes 98312 | tf_op jit(solution)/shard_map/ppermute | solution.py:235
  123.0 7.0 %collective-permute-start.21 = (f32[32,256]{1,0:T(8,128)S(1)}, f32[32,256]{1,0:T(8,128)S(1)}, u32[]{:S(2)}, u32[]{:S(2)}) collective-permute-start(f32[32,256]{1,0:T(8,128)S(1)} %get-tuple-element.97), channel_id=1, source_target_pairs={{0,252},{4,0},{8,4},{12,8},{16,12},{20,16},{24,20},{28,24},{32,28}... | collective-permute-start | bytes 98312 | tf_op jit(solution)/shard_map/ppermute | solution.py:235
  131.0 7.1 %collective-permute-start.22 = (f32[32,256]{1,0:T(8,128)S(1)}, f32[32,256]{1,0:T(8,128)S(1)}, u32[]{:S(2)}, u32[]{:S(2)}) collective-permute-start(f32[32,256]{1,0:T(8,128)S(1)} %get-tuple-element.99), channel_id=1, source_target_pairs={{0,4},{4,8},{8,12},{12,16},{16,20},{20,24},{24,28},{28,32},{32,36}... | collective-permute-start | bytes 98312 | tf_op jit(solution)/shard_map/ppermute | solution.py:235
  131.0 7.0 %collective-permute-start.23 = (f32[32,256]{1,0:T(8,128)S(1)}, f32[32,256]{1,0:T(8,128)S(1)}, u32[]{:S(2)}, u32[]{:S(2)}) collective-permute-start(f32[32,256]{1,0:T(8,128)S(1)} %get-tuple-element.100), channel_id=1, source_target_pairs={{0,252},{4,0},{8,4},{12,8},{16,12},{20,16},{24,20},{28,24},{32,28}... | collective-permute-start | bytes 98312 | tf_op jit(solution)/shard_map/ppermute | solution.py:235
  141.9 20.9 %all-to-all-start.2 = ((f32[64,4,128]{2,1,0:T(4,128)}), f32[64,4,128]{2,1,0:T(4,128)S(1)}, u32[]{:S(2)}, u32[]{:S(2)}) async-start(f32[64,4,128]{2,1,0:T(4,128)} %get-tuple-element.103), calls=%async_computation.2 | async-start | bytes 262144 | tf_op jit(solution)/shard_map/all_to_all | solution.py:248
  163.2 16.5 %collective-permute-start.24 = (f32[2,32,128]{2,1,0:T(8,128)S(1)}, f32[2,32,128]{2,1,0:T(8,128)S(1)}, u32[]{:S(2)}, u32[]{:S(2)}) collective-permute-start(f32[2,32,128]{2,1,0:T(8,128)S(1)} %get-tuple-element.113), channel_id=1, source_target_pairs={{0,1},{1,0},{2,3},{3,2},{4,5},{5,4},{6,7},{7,6},{8,9},{9,8},{10,11... | collective-permute-start | bytes 98312 | tf_op jit(solution)/shard_map/ppermute | solution.py:279

commit v2 on v1

--- a/solution.py
+++ b/solution.py
@@ -34,8 +34,23 @@
 
 def split(value):
     high = value.astype(jnp.bfloat16)
-    low = (value - high.astype(jnp.float32)).astype(jnp.bfloat16)
-    return high, low
+    value = value - high.astype(jnp.float32)
+    middle = value.astype(jnp.bfloat16)
+    low = (value - middle.astype(jnp.float32)).astype(jnp.bfloat16)
+    return high, middle, low
+
+
+def product(vector, high, middle, low):
+    parts = split(vector)
+    first = jnp.dot(
+        jnp.concatenate(parts, 0), high[...], preferred_element_type=jnp.float32
+    )
+    second = jnp.dot(
+        jnp.concatenate(parts[:2], 0), middle[...], preferred_element_type=jnp.float32
+    )
+    third = jnp.dot(parts[0], low[...], preferred_element_type=jnp.float32)
+    small = first[2 * COLS :] + second[COLS:] + third
+    return first[:COLS] + (first[COLS : 2 * COLS] + second[:COLS] + small)
 
 
 def write_sends(lists, vector, to_next, to_previous):
@@ -45,7 +60,8 @@
             target[:, slot * BS : (slot + 1) * BS] = vector[:, pl.ds(start, BS)]
 
 
-def operator_kernel(cols, blocks, high, low, dense):
+def operator_kernel(cols, blocks, *refs):
+    own, received, dense = refs[:3], refs[3:6], refs[6]
     dense[...] = jnp.zeros_like(dense)
     for row in range(NB):
         for slot in range(blocks.shape[1]):
@@ -61,7 +77,10 @@
             value = dense[place]
             if row == column:
                 value = value - CENTER * unit
-            high[place], low[place] = split(value * (1.0 / RADIUS))
+            targets = own if column < NB else received
+            start = (column % NB) * BS
+            for target, part in zip(targets, split(value * (1.0 / RADIUS))):
+                target[start : start + BS, row * BS : (row + 1) * BS] = part
 
 
 def start_kernel(lists, core, gathered, vector, to_next, to_previous):
@@ -70,14 +89,14 @@
     write_sends(lists, vector, to_next, to_previous)
 
 
-def step_kernel(lists, vector, from_previous, from_next, high, low, result, to_next, to_previous):
-    extended = jnp.concatenate([vector[...], from_previous[...], from_next[...]], 1)
-    top, rest = split(extended)
-    first = jnp.dot(
-        jnp.concatenate([top, rest], 0), high[...], preferred_element_type=jnp.float32
-    )
-    second = jnp.dot(top, low[...], preferred_element_type=jnp.float32)
-    result[...] = first[:COLS] + (first[COLS:] + second)
+def own_kernel(vector, high, middle, low, partial):
+    partial[...] = product(vector[...], high, middle, low)
+
+
+def step_kernel(lists, partial, from_previous, from_next, *refs):
+    parts, (result, to_next, to_previous) = refs[:3], refs[3:]
+    received = jnp.concatenate([from_previous[...], from_next[...]], 1)
+    result[...] = partial[...] + product(received, *parts)
     write_sends(lists, result, to_next, to_previous)
 
 
@@ -197,7 +216,7 @@
         residual[:, place] = combined_tile(left, vectors, tile)
 
 
-def call(kernel, out_shape, smem, vmem, scratch=()):
+def call(kernel, out_shape, smem, vmem, scratch=(), flops=10**6):
     return pl.pallas_call(
         kernel,
         out_shape=out_shape,
@@ -205,6 +224,7 @@
         out_specs=jax.tree.map(lambda unused: VMEM, out_shape),
         scratch_shapes=scratch,
         compiler_params=PARAMS,
+        cost_estimate=pl.CostEstimate(flops=flops, bytes_accessed=2**20, transcendentals=0),
     )(*smem, *vmem)
 
 
@@ -216,9 +236,9 @@
     vector_shape = f32(COLS, ROWS)
     halo_shape = f32(COLS, HALO * BS)
     gram_shape = f32(subs, GRAM_ROWS, BS)
-    high, low = call(
+    operator = call(
         operator_kernel,
-        (bf16(EXT * BS, ROWS), bf16(EXT * BS, ROWS)),
+        (bf16(ROWS, ROWS),) * 6,
         [block_cols],
         [blocks],
         [pltpu.VMEM((EXT * BS, ROWS), jnp.float32)],
@@ -237,11 +257,12 @@
     def step(vector, to_next, to_previous):
         from_previous = passed(to_next, 1)
         from_next = passed(to_previous, -1)
+        partial = call(own_kernel, vector_shape, [], [vector, *operator[:3]], flops=10**9)
         return call(
             step_kernel,
             (vector_shape, halo_shape, halo_shape),
             [lists],
-            [vector, from_previous, from_next, high, low],
+            [partial, from_previous, from_next, *operator[3:]],
         )
 
     def exchanged(gram):

time: 181 us -> 173 us (0.956)
  starting transfers between devices: 119 us -> 108 us
  local copies, waits for them, and re-layouts: 3.5 us -> 10.1 us
  waiting for transfers between devices: 24.7 us -> 18.1 us
  Pallas kernels: 21.7 us -> 25.2 us
    all_to_all x3, starting transfers between devices: 30.9 us -> 22.7 us  [exchanged(): return lax.all_to_all(gram, 'sub', 0, 0)]
    ppermute x24, waiting for transfers between devices: 14.1 us -> 7.44 us  [passed(): lax.ppermute(value, 'sub', [(i, (i + by) % subs) for i in range(subs)])]
    unnamed x8 -> x24, local copies, waits for them, and re-layouts: 2.87 us -> 9.45 us
    pallas_call x18 -> x30, Pallas kernels: 21.7 us -> 25.2 us  [call(): pl.pallas_call(kernel, out_shape=out_shape, in_specs=[SMEM] * len(smem) +...]
  transfers between devices with their start and end apart: 28 -> 28, of which waited for: 13 -> 9; matrix products, arithmetic and copies ran while one was open for 0% -> 0% of each run, Pallas kernels for 6% -> 9%
where the time goes in v2:
time: 173 us
  starting transfers between devices  108 us (62%)
  Pallas kernels  25.2 us (15%)
  waiting for transfers between devices  18.1 us (10%)
  blocking collectives  10.2 us (6%)
  local copies, waits for them, and re-layouts  10.1 us (6%)
    ppermute x24, starting transfers between devices, passed(): lax.ppermute(value, 'sub', [(i, (i + by) % subs) for i in range(subs)])  71.4 us
    pallas_call x30, Pallas kernels, call(): pl.pallas_call(kernel, out_shape=out_shape, in_specs=[SMEM] * len(smem) +...  25.2 us
    all_to_all x3, starting transfers between devices, exchanged(): return lax.all_to_all(gram, 'sub', 0, 0)  22.7 us
    ppermute x1, starting transfers between devices, on_device(): arrived = lax.ppermute(other, 'fold', [(0, 1), (1, 0), (2, 3), (3, 2)])  14 us
    all_gather x1, blocking collectives, on_device(): gathered = lax.all_gather(right_side.T, 'fold', axis=1, tiled=True)  10.2 us
    all_to_all x3, waiting for transfers between devices, exchanged(): return lax.all_to_all(gram, 'sub', 0, 0)  9.8 us
    unnamed x24, local copies, waits for them, and re-layouts  9.45 us
    ppermute x24, waiting for transfers between devices, passed(): lax.ppermute(value, 'sub', [(i, (i + by) % subs) for i in range(subs)])  7.44 us
  transfers between devices with their start and end apart: 28, of which 9 were waited for; matrix products, arithmetic and copies ran while one was open for 0% of the time, Pallas kernels for 9%

profile of v2, /device:TPU:1, one launch (start us, length us, event | category | flops | bytes accessed | tf_op | source)
XLA Modules:
  0.0 172.7 jit_solution(10083918016928319880)
XLA Ops:
  0.6 10.2 %all_gather.3.gathered = f32[64,512]{1,0:T(8,128)S(1)} all-gather(f32[64,128]{1,0:T(8,128)} %bitcast.30), channel_id=1, replica_groups=mesh['sub'=64,'fold'=4] {'fold'}, dimensions={1}, use_global_device_ids=true | all-gather | bytes 163840 | tf_op jit(solution)/shard_map/all_gather | solution.py:246
  12.2 7.3 %collective-permute-start.1 = (f32[32,256]{1,0:T(8,128)S(1)}, f32[32,256]{1,0:T(8,128)S(1)}, u32[]{:S(2)}, u32[]{:S(2)}) collective-permute-start(f32[32,256]{1,0:T(8,128)S(1)} %get-tuple-element.66), channel_id=1, source_target_pairs={{0,252},{4,0},{8,4},{12,8},{16,12},{20,16},{24,20},{28,24},{32,28}... | collective-permute-start | bytes 98312 | tf_op jit(solution)/shard_map/ppermute | solution.py:255
  19.5 1.5 copy-done
  21.7 2.1 %shard_map.60 = (bf16[512,512]{1,0:T(8,128)(2,1)S(1)}, bf16[512,512]{1,0:T(8,128)(2,1)S(1)}, bf16[512,512]{1,0:T(8,128)(2,1)S(1)}, bf16[512,512]{1,0:T(8,128)(2,...) custom-call(s32[4,7]{1,0:T(4,128)S(1)} %copy-done.3, f32[4,7,128,128]{3,2,1,0:T(8,128)S(1)} %copy-done), custom_call_target="tpu_custom_call" | custom-call | flops 1000000 | bytes 1048576 | tf_op jit(solution)/shard_map/pallas_call | solution.py:220
  25.5 5.7 %collective-permute-start.3 = (f32[32,256]{1,0:T(8,128)S(1)}, f32[32,256]{1,0:T(8,128)S(1)}, u32[]{:S(2)}, u32[]{:S(2)}) collective-permute-start(f32[32,256]{1,0:T(8,128)S(1)} %get-tuple-element.72), channel_id=1, source_target_pairs={{0,252},{4,0},{8,4},{12,8},{16,12},{20,16},{24,20},{28,24},{32,28}... | collective-permute-start | bytes 98312 | tf_op jit(solution)/shard_map/ppermute | solution.py:255
  33.5 5.8 %collective-permute-start.5 = (f32[32,256]{1,0:T(8,128)S(1)}, f32[32,256]{1,0:T(8,128)S(1)}, u32[]{:S(2)}, u32[]{:S(2)}) collective-permute-start(f32[32,256]{1,0:T(8,128)S(1)} %get-tuple-element.75), channel_id=1, source_target_pairs={{0,252},{4,0},{8,4},{12,8},{16,12},{20,16},{24,20},{28,24},{32,28}... | collective-permute-start | bytes 98312 | tf_op jit(solution)/shard_map/ppermute | solution.py:255
  41.6 5.8 %collective-permute-start.7 = (f32[32,256]{1,0:T(8,128)S(1)}, f32[32,256]{1,0:T(8,128)S(1)}, u32[]{:S(2)}, u32[]{:S(2)}) collective-permute-start(f32[32,256]{1,0:T(8,128)S(1)} %get-tuple-element.78), channel_id=1, source_target_pairs={{0,252},{4,0},{8,4},{12,8},{16,12},{20,16},{24,20},{28,24},{32,28}... | collective-permute-start | bytes 98312 | tf_op jit(solution)/shard_map/ppermute | solution.py:255
  49.7 5.8 %collective-permute-start.9 = (f32[32,256]{1,0:T(8,128)S(1)}, f32[32,256]{1,0:T(8,128)S(1)}, u32[]{:S(2)}, u32[]{:S(2)}) collective-permute-start(f32[32,256]{1,0:T(8,128)S(1)} %get-tuple-element.81), channel_id=1, source_target_pairs={{0,252},{4,0},{8,4},{12,8},{16,12},{20,16},{24,20},{28,24},{32,28}... | collective-permute-start | bytes 98312 | tf_op jit(solution)/shard_map/ppermute | solution.py:255
  55.9 1.2 shard_map.69
  57.0 5.8 %all-to-all-start = ((f32[64,4,128]{2,1,0:T(4,128)}), f32[64,4,128]{2,1,0:T(4,128)S(1)}, u32[]{:S(2)}, u32[]{:S(2)}) async-start(f32[64,4,128]{2,1,0:T(4,128)} %shard_map.69), calls=%async_computation | async-start | bytes 262144 | tf_op jit(solution)/shard_map/all_to_all | solution.py:269
  63.8 1.1 collective-permute-start.10
  64.9 4.7 %collective-permute-start.11 = (f32[32,256]{1,0:T(8,128)S(1)}, f32[32,256]{1,0:T(8,128)S(1)}, u32[]{:S(2)}, u32[]{:S(2)}) collective-permute-start(f32[32,256]{1,0:T(8,128)S(1)} %get-tuple-element.84), channel_id=1, source_target_pairs={{0,252},{4,0},{8,4},{12,8},{16,12},{20,16},{24,20},{28,24},{32,28}... | collective-permute-start | bytes 98312 | tf_op jit(solution)/shard_map/ppermute | solution.py:255
  69.5 1.0 copy-done.5
  70.6 1.0 copy-done.9
  73.0 5.7 %collective-permute-start.13 = (f32[32,256]{1,0:T(8,128)S(1)}, f32[32,256]{1,0:T(8,128)S(1)}, u32[]{:S(2)}, u32[]{:S(2)}) collective-permute-start(f32[32,256]{1,0:T(8,128)S(1)} %get-tuple-element.87), channel_id=1, source_target_pairs={{0,252},{4,0},{8,4},{12,8},{16,12},{20,16},{24,20},{28,24},{32,28}... | collective-permute-start | bytes 98312 | tf_op jit(solution)/shard_map/ppermute | solution.py:255
  81.0 5.9 %collective-permute-start.15 = (f32[32,256]{1,0:T(8,128)S(1)}, f32[32,256]{1,0:T(8,128)S(1)}, u32[]{:S(2)}, u32[]{:S(2)}) collective-permute-start(f32[32,256]{1,0:T(8,128)S(1)} %get-tuple-element.90), channel_id=1, source_target_pairs={{0,252},{4,0},{8,4},{12,8},{16,12},{20,16},{24,20},{28,24},{32,28}... | collective-permute-start | bytes 98312 | tf_op jit(solution)/shard_map/ppermute | solution.py:255
  88.1 1.6 shard_map.77
  89.7 2.2 %shard_map.78 = (f32[32,512]{1,0:T(8,128)S(1)}, f32[32,512]{1,0:T(8,128)S(1)}, f32[32,512]{1,0:T(8,128)S(1)}, f32[32,512]{1,0:T(8,128)S(1)}, f32[32,512]{1,0:T(8...) custom-call(s32[2,2]{1,0:T(2,128)S(1)} %bitcast.22, ...), custom_call_target="tpu_custom_call" | custom-call | flops 1000000 | bytes 1048576 | tf_op jit(solution)/shard_map/pallas_call | solution.py:220
  91.9 5.8 %collective-permute-start.17 = (f32[32,256]{1,0:T(8,128)S(1)}, f32[32,256]{1,0:T(8,128)S(1)}, u32[]{:S(2)}, u32[]{:S(2)}) collective-permute-start(f32[32,256]{1,0:T(8,128)S(1)} %get-tuple-element.99), channel_id=1, source_target_pairs={{0,252},{4,0},{8,4},{12,8},{16,12},{20,16},{24,20},{28,24},{32,28}... | collective-permute-start | bytes 98312 | tf_op jit(solution)/shard_map/ppermute | solution.py:255
  98.7 1.0 copy-done.10
  100.1 7.2 %all-to-all-start.1 = ((f32[64,4,128]{2,1,0:T(4,128)}), f32[64,4,128]{2,1,0:T(4,128)S(1)}, u32[]{:S(2)}, u32[]{:S(2)}) async-start(f32[64,4,128]{2,1,0:T(4,128)} %get-tuple-element.92), calls=%async_computation.1 | async-start | bytes 262144 | tf_op jit(solution)/shard_map/all_to_all | solution.py:269
  108.2 1.1 collective-permute-start.18
  109.3 4.7 %collective-permute-start.19 = (f32[32,256]{1,0:T(8,128)S(1)}, f32[32,256]{1,0:T(8,128)S(1)}, u32[]{:S(2)}, u32[]{:S(2)}) collective-permute-start(f32[32,256]{1,0:T(8,128)S(1)} %get-tuple-element.102), channel_id=1, source_target_pairs={{0,252},{4,0},{8,4},{12,8},{16,12},{20,16},{24,20},{28,24},{32,28}... | collective-permute-start | bytes 98312 | tf_op jit(solution)/shard_map/ppermute | solution.py:255
  115.1 1.0 copy-done.11
  117.5 5.7 %collective-permute-start.21 = (f32[32,256]{1,0:T(8,128)S(1)}, f32[32,256]{1,0:T(8,128)S(1)}, u32[]{:S(2)}, u32[]{:S(2)}) collective-permute-start(f32[32,256]{1,0:T(8,128)S(1)} %get-tuple-element.105), channel_id=1, source_target_pairs={{0,252},{4,0},{8,4},{12,8},{16,12},{20,16},{24,20},{28,24},{32,28}... | collective-permute-start | bytes 98312 | tf_op jit(solution)/shard_map/ppermute | solution.py:255
  123.5 1.9 %collective-permute-done.20.from_previous = f32[32,256]{1,0:T(8,128)S(1)} collective-permute-done((f32[32,256]{1,0:T(8,128)S(1)}, f32[32,256]{1,0:T(8,128)S(1)}, u32[]{:S(2)}, u32[]{:S(2)}) %collective-permute-start.20) | collective-permute-done | bytes 32800 | tf_op jit(solution)/shard_map/ppermute | solution.py:255
  126.5 5.7 %collective-permute-start.23 = (f32[32,256]{1,0:T(8,128)S(1)}, f32[32,256]{1,0:T(8,128)S(1)}, u32[]{:S(2)}, u32[]{:S(2)}) collective-permute-start(f32[32,256]{1,0:T(8,128)S(1)} %get-tuple-element.108), channel_id=1, source_target_pairs={{0,252},{4,0},{8,4},{12,8},{16,12},{20,16},{24,20},{28,24},{32,28}... | collective-permute-start | bytes 98312 | tf_op jit(solution)/shard_map/ppermute | solution.py:255
  133.5 1.6 shard_map.86
  135.0 2.2 %shard_map.87 = (f32[32,512]{1,0:T(8,128)S(1)}, f32[32,512]{1,0:T(8,128)S(1)}, f32[32,512]{1,0:T(8,128)S(1)}, f32[32,512]{1,0:T(8,128)S(1)}, f32[32,512]{1,0:T(8...) custom-call(s32[2,2]{1,0:T(2,128)S(1)} %bitcast.27, ...), custom_call_target="tpu_custom_call" | custom-call | flops 1000000 | bytes 1048576 | tf_op jit(solution)/shard_map/pallas_call | solution.py:220
  137.2 9.7 %all-to-all-start.2 = ((f32[64,4,128]{2,1,0:T(4,128)}), f32[64,4,128]{2,1,0:T(4,128)S(1)}, u32[]{:S(2)}, u32[]{:S(2)}) async-start(f32[64,4,128]{2,1,0:T(4,128)} %get-tuple-element.111), calls=%async_computation.2 | async-start | bytes 262144 | tf_op jit(solution)/shard_map/all_to_all | solution.py:269
  146.9 9.8 %all-to-all-done.2.gathered = f32[64,4,128]{2,1,0:T(4,128)S(1)} async-done(((f32[64,4,128]{2,1,0:T(4,128)}), f32[64,4,128]{2,1,0:T(4,128)S(1)}, u32[]{:S(2)}, u32[]{:S(2)}) %all-to-all-start.2) | async-done | bytes 131104 | tf_op jit(solution)/shard_map/all_to_all | solution.py:269
  157.1 14.0 %collective-permute-start.24 = (f32[2,32,128]{2,1,0:T(8,128)S(1)}, f32[2,32,128]{2,1,0:T(8,128)S(1)}, u32[]{:S(2)}, u32[]{:S(2)}) collective-permute-start(f32[2,32,128]{2,1,0:T(8,128)S(1)} %get-tuple-element.121), channel_id=1, source_target_pairs={{0,1},{1,0},{2,3},{3,2},{4,5},{5,4},{6,7},{7,6},{8,9},{9,8},{10,11... | collective-permute-start | bytes 98312 | tf_op jit(solution)/shard_map/ppermute | solution.py:300
  (82 shorter events, 26.1 us)
Async XLA Ops:
  12.1 12.0 %collective-permute-start = (f32[32,256]{1,0:T(8,128)S(1)}, f32[32,256]{1,0:T(8,128)S(1)}, u32[]{:S(2)}, u32[]{:S(2)}) collective-permute-start(f32[32,256]{1,0:T(8,128)S(1)} %get-tuple-element.65), channel_id=1, source_target_pairs={{0,4},{4,8},{8,12},{12,16},{16,20},{20,24},{24,28},{28,32},{32,36}... | collective-permute-start | bytes 98312 | tf_op jit(solution)/shard_map/ppermute | solution.py:255
  12.2 12.0 %collective-permute-start.1 = (f32[32,256]{1,0:T(8,128)S(1)}, f32[32,256]{1,0:T(8,128)S(1)}, u32[]{:S(2)}, u32[]{:S(2)}) collective-permute-start(f32[32,256]{1,0:T(8,128)S(1)} %get-tuple-element.66), channel_id=1, source_target_pairs={{0,252},{4,0},{8,4},{12,8},{16,12},{20,16},{24,20},{28,24},{32,28}... | collective-permute-start | bytes 98312 | tf_op jit(solution)/shard_map/ppermute | solution.py:255
  19.5 1.5 copy-start
  23.8 31.8 %copy-start.4 = (bf16[512,512]{1,0:T(8,128)(2,1)}, bf16[512,512]{1,0:T(8,128)(2,1)S(1)}, u32[]{:S(2)}) copy-start(bf16[512,512]{1,0:T(8,128)(2,1)S(1)} %get-tuple-element.63.middle) | copy-start | bytes 1572868
  23.8 31.8 %copy-start.8 = (bf16[512,512]{1,0:T(8,128)(2,1)}, bf16[512,512]{1,0:T(8,128)(2,1)S(1)}, u32[]{:S(2)}) copy-start(bf16[512,512]{1,0:T(8,128)(2,1)S(1)} %get-tuple-element.64.low) | copy-start | bytes 1572868
  25.4 7.1 %collective-permute-start.2 = (f32[32,256]{1,0:T(8,128)S(1)}, f32[32,256]{1,0:T(8,128)S(1)}, u32[]{:S(2)}, u32[]{:S(2)}) collective-permute-start(f32[32,256]{1,0:T(8,128)S(1)} %get-tuple-element.71), channel_id=1, source_target_pairs={{0,4},{4,8},{8,12},{12,16},{16,20},{20,24},{24,28},{28,32},{32,36}... | collective-permute-start | bytes 98312 | tf_op jit(solution)/shard_map/ppermute | solution.py:255
  25.5 7.0 %collective-permute-start.3 = (f32[32,256]{1,0:T(8,128)S(1)}, f32[32,256]{1,0:T(8,128)S(1)}, u32[]{:S(2)}, u32[]{:S(2)}) collective-permute-start(f32[32,256]{1,0:T(8,128)S(1)} %get-tuple-element.72), channel_id=1, source_target_pairs={{0,252},{4,0},{8,4},{12,8},{16,12},{20,16},{24,20},{28,24},{32,28}... | collective-permute-start | bytes 98312 | tf_op jit(solution)/shard_map/ppermute | solution.py:255
  33.4 7.1 %collective-permute-start.4 = (f32[32,256]{1,0:T(8,128)S(1)}, f32[32,256]{1,0:T(8,128)S(1)}, u32[]{:S(2)}, u32[]{:S(2)}) collective-permute-start(f32[32,256]{1,0:T(8,128)S(1)} %get-tuple-element.74), channel_id=1, source_target_pairs={{0,4},{4,8},{8,12},{12,16},{16,20},{20,24},{24,28},{28,32},{32,36}... | collective-permute-start | bytes 98312 | tf_op jit(solution)/shard_map/ppermute | solution.py:255
  33.5 7.0 %collective-permute-start.5 = (f32[32,256]{1,0:T(8,128)S(1)}, f32[32,256]{1,0:T(8,128)S(1)}, u32[]{:S(2)}, u32[]{:S(2)}) collective-permute-start(f32[32,256]{1,0:T(8,128)S(1)} %get-tuple-element.75), channel_id=1, source_target_pairs={{0,252},{4,0},{8,4},{12,8},{16,12},{20,16},{24,20},{28,24},{32,28}... | collective-permute-start | bytes 98312 | tf_op jit(solution)/shard_map/ppermute | solution.py:255
  41.5 7.1 %collective-permute-start.6 = (f32[32,256]{1,0:T(8,128)S(1)}, f32[32,256]{1,0:T(8,128)S(1)}, u32[]{:S(2)}, u32[]{:S(2)}) collective-permute-start(f32[32,256]{1,0:T(8,128)S(1)} %get-tuple-element.77), channel_id=1, source_target_pairs={{0,4},{4,8},{8,12},{12,16},{16,20},{20,24},{24,28},{28,32},{32,36}... | collective-permute-start | bytes 98312 | tf_op jit(solution)/shard_map/ppermute | solution.py:255
  41.6 7.1 %collective-permute-start.7 = (f32[32,256]{1,0:T(8,128)S(1)}, f32[32,256]{1,0:T(8,128)S(1)}, u32[]{:S(2)}, u32[]{:S(2)}) collective-permute-start(f32[32,256]{1,0:T(8,128)S(1)} %get-tuple-element.78), channel_id=1, source_target_pairs={{0,252},{4,0},{8,4},{12,8},{16,12},{20,16},{24,20},{28,24},{32,28}... | collective-permute-start | bytes 98312 | tf_op jit(solution)/shard_map/ppermute | solution.py:255
  49.6 13.2 %collective-permute-start.8 = (f32[32,256]{1,0:T(8,128)S(1)}, f32[32,256]{1,0:T(8,128)S(1)}, u32[]{:S(2)}, u32[]{:S(2)}) collective-permute-start(f32[32,256]{1,0:T(8,128)S(1)} %get-tuple-element.80), channel_id=1, source_target_pairs={{0,4},{4,8},{8,12},{12,16},{16,20},{20,24},{24,28},{28,32},{32,36}... | collective-permute-start | bytes 98312 | tf_op jit(solution)/shard_map/ppermute | solution.py:255
  49.7 13.1 %collective-permute-start.9 = (f32[32,256]{1,0:T(8,128)S(1)}, f32[32,256]{1,0:T(8,128)S(1)}, u32[]{:S(2)}, u32[]{:S(2)}) collective-permute-start(f32[32,256]{1,0:T(8,128)S(1)} %get-tuple-element.81), channel_id=1, source_target_pairs={{0,252},{4,0},{8,4},{12,8},{16,12},{20,16},{24,20},{28,24},{32,28}... | collective-permute-start | bytes 98312 | tf_op jit(solution)/shard_map/ppermute | solution.py:255
  57.0 32.6 %all-to-all-start = ((f32[64,4,128]{2,1,0:T(4,128)}), f32[64,4,128]{2,1,0:T(4,128)S(1)}, u32[]{:S(2)}, u32[]{:S(2)}) async-start(f32[64,4,128]{2,1,0:T(4,128)} %shard_map.69), calls=%async_computation | async-start | bytes 262144 | tf_op jit(solution)/shard_map/all_to_all | solution.py:269
  63.8 8.2 %collective-permute-start.10 = (f32[32,256]{1,0:T(8,128)S(1)}, f32[32,256]{1,0:T(8,128)S(1)}, u32[]{:S(2)}, u32[]{:S(2)}) collective-permute-start(f32[32,256]{1,0:T(8,128)S(1)} %get-tuple-element.83), channel_id=1, source_target_pairs={{0,4},{4,8},{8,12},{12,16},{16,20},{20,24},{24,28},{28,32},{32,36}... | collective-permute-start | bytes 98312 | tf_op jit(solution)/shard_map/ppermute | solution.py:255
  64.9 7.1 %collective-permute-start.11 = (f32[32,256]{1,0:T(8,128)S(1)}, f32[32,256]{1,0:T(8,128)S(1)}, u32[]{:S(2)}, u32[]{:S(2)}) collective-permute-start(f32[32,256]{1,0:T(8,128)S(1)} %get-tuple-element.84), channel_id=1, source_target_pairs={{0,252},{4,0},{8,4},{12,8},{16,12},{20,16},{24,20},{28,24},{32,28}... | collective-permute-start | bytes 98312 | tf_op jit(solution)/shard_map/ppermute | solution.py:255
  69.5 1.0 copy-start.5
  72.9 7.1 %collective-permute-start.12 = (f32[32,256]{1,0:T(8,128)S(1)}, f32[32,256]{1,0:T(8,128)S(1)}, u32[]{:S(2)}, u32[]{:S(2)}) collective-permute-start(f32[32,256]{1,0:T(8,128)S(1)} %get-tuple-element.86), channel_id=1, source_target_pairs={{0,4},{4,8},{8,12},{12,16},{16,20},{20,24},{24,28},{28,32},{32,36}... | collective-permute-start | bytes 98312 | tf_op jit(solution)/shard_map/ppermute | solution.py:255
  73.0 7.0 %collective-permute-start.13 = (f32[32,256]{1,0:T(8,128)S(1)}, f32[32,256]{1,0:T(8,128)S(1)}, u32[]{:S(2)}, u32[]{:S(2)}) collective-permute-start(f32[32,256]{1,0:T(8,128)S(1)} %get-tuple-element.87), channel_id=1, source_target_pairs={{0,252},{4,0},{8,4},{12,8},{16,12},{20,16},{24,20},{28,24},{32,28}... | collective-permute-start | bytes 98312 | tf_op jit(solution)/shard_map/ppermute | solution.py:255
  80.9 7.2 %collective-permute-start.14 = (f32[32,256]{1,0:T(8,128)S(1)}, f32[32,256]{1,0:T(8,128)S(1)}, u32[]{:S(2)}, u32[]{:S(2)}) collective-permute-start(f32[32,256]{1,0:T(8,128)S(1)} %get-tuple-element.89), channel_id=1, source_target_pairs={{0,4},{4,8},{8,12},{12,16},{16,20},{20,24},{24,28},{28,32},{32,36}... | collective-permute-start | bytes 98312 | tf_op jit(solution)/shard_map/ppermute | solution.py:255
  81.0 7.1 %collective-permute-start.15 = (f32[32,256]{1,0:T(8,128)S(1)}, f32[32,256]{1,0:T(8,128)S(1)}, u32[]{:S(2)}, u32[]{:S(2)}) collective-permute-start(f32[32,256]{1,0:T(8,128)S(1)} %get-tuple-element.90), channel_id=1, source_target_pairs={{0,252},{4,0},{8,4},{12,8},{16,12},{20,16},{24,20},{28,24},{32,28}... | collective-permute-start | bytes 98312 | tf_op jit(solution)/shard_map/ppermute | solution.py:255
  91.9 15.4 %collective-permute-start.16 = (f32[32,256]{1,0:T(8,128)S(1)}, f32[32,256]{1,0:T(8,128)S(1)}, u32[]{:S(2)}, u32[]{:S(2)}) collective-permute-start(f32[32,256]{1,0:T(8,128)S(1)} %get-tuple-element.98), channel_id=1, source_target_pairs={{0,4},{4,8},{8,12},{12,16},{16,20},{20,24},{24,28},{28,32},{32,36}... | collective-permute-start | bytes 98312 | tf_op jit(solution)/shard_map/ppermute | solution.py:255
  91.9 15.4 %collective-permute-start.17 = (f32[32,256]{1,0:T(8,128)S(1)}, f32[32,256]{1,0:T(8,128)S(1)}, u32[]{:S(2)}, u32[]{:S(2)}) collective-permute-start(f32[32,256]{1,0:T(8,128)S(1)} %get-tuple-element.99), channel_id=1, source_target_pairs={{0,252},{4,0},{8,4},{12,8},{16,12},{20,16},{24,20},{28,24},{32,28}... | collective-permute-start | bytes 98312 | tf_op jit(solution)/shard_map/ppermute | solution.py:255
  100.1 35.0 %all-to-all-start.1 = ((f32[64,4,128]{2,1,0:T(4,128)}), f32[64,4,128]{2,1,0:T(4,128)S(1)}, u32[]{:S(2)}, u32[]{:S(2)}) async-start(f32[64,4,128]{2,1,0:T(4,128)} %get-tuple-element.92), calls=%async_computation.1 | async-start | bytes 262144 | tf_op jit(solution)/shard_map/all_to_all | solution.py:269
  108.2 8.2 %collective-permute-start.18 = (f32[32,256]{1,0:T(8,128)S(1)}, f32[32,256]{1,0:T(8,128)S(1)}, u32[]{:S(2)}, u32[]{:S(2)}) collective-permute-start(f32[32,256]{1,0:T(8,128)S(1)} %get-tuple-element.101), channel_id=1, source_target_pairs={{0,4},{4,8},{8,12},{12,16},{16,20},{20,24},{24,28},{28,32},{32,36}... | collective-permute-start | bytes 98312 | tf_op jit(solution)/shard_map/ppermute | solution.py:255
  109.3 7.1 %collective-permute-start.19 = (f32[32,256]{1,0:T(8,128)S(1)}, f32[32,256]{1,0:T(8,128)S(1)}, u32[]{:S(2)}, u32[]{:S(2)}) collective-permute-start(f32[32,256]{1,0:T(8,128)S(1)} %get-tuple-element.102), channel_id=1, source_target_pairs={{0,252},{4,0},{8,4},{12,8},{16,12},{20,16},{24,20},{28,24},{32,28}... | collective-permute-start | bytes 98312 | tf_op jit(solution)/shard_map/ppermute | solution.py:255
  117.4 8.1 %collective-permute-start.20 = (f32[32,256]{1,0:T(8,128)S(1)}, f32[32,256]{1,0:T(8,128)S(1)}, u32[]{:S(2)}, u32[]{:S(2)}) collective-permute-start(f32[32,256]{1,0:T(8,128)S(1)} %get-tuple-element.104), channel_id=1, source_target_pairs={{0,4},{4,8},{8,12},{12,16},{16,20},{20,24},{24,28},{28,32},{32,36}... | collective-permute-start | bytes 98312 | tf_op jit(solution)/shard_map/ppermute | solution.py:255
  117.5 8.0 %collective-permute-start.21 = (f32[32,256]{1,0:T(8,128)S(1)}, f32[32,256]{1,0:T(8,128)S(1)}, u32[]{:S(2)}, u32[]{:S(2)}) collective-permute-start(f32[32,256]{1,0:T(8,128)S(1)} %get-tuple-element.105), channel_id=1, source_target_pairs={{0,252},{4,0},{8,4},{12,8},{16,12},{20,16},{24,20},{28,24},{32,28}... | collective-permute-start | bytes 98312 | tf_op jit(solution)/shard_map/ppermute | solution.py:255
  126.4 7.1 %collective-permute-start.22 = (f32[32,256]{1,0:T(8,128)S(1)}, f32[32,256]{1,0:T(8,128)S(1)}, u32[]{:S(2)}, u32[]{:S(2)}) collective-permute-start(f32[32,256]{1,0:T(8,128)S(1)} %get-tuple-element.107), channel_id=1, source_target_pairs={{0,4},{4,8},{8,12},{12,16},{16,20},{20,24},{24,28},{28,32},{32,36}... | collective-permute-start | bytes 98312 | tf_op jit(solution)/shard_map/ppermute | solution.py:255
  126.5 7.0 %collective-permute-start.23 = (f32[32,256]{1,0:T(8,128)S(1)}, f32[32,256]{1,0:T(8,128)S(1)}, u32[]{:S(2)}, u32[]{:S(2)}) collective-permute-start(f32[32,256]{1,0:T(8,128)S(1)} %get-tuple-element.108), channel_id=1, source_target_pairs={{0,252},{4,0},{8,4},{12,8},{16,12},{20,16},{24,20},{28,24},{32,28}... | collective-permute-start | bytes 98312 | tf_op jit(solution)/shard_map/ppermute | solution.py:255
  137.2 19.5 %all-to-all-start.2 = ((f32[64,4,128]{2,1,0:T(4,128)}), f32[64,4,128]{2,1,0:T(4,128)S(1)}, u32[]{:S(2)}, u32[]{:S(2)}) async-start(f32[64,4,128]{2,1,0:T(4,128)} %get-tuple-element.111), calls=%async_computation.2 | async-start | bytes 262144 | tf_op jit(solution)/shard_map/all_to_all | solution.py:269
  157.1 14.9 %collective-permute-start.24 = (f32[2,32,128]{2,1,0:T(8,128)S(1)}, f32[2,32,128]{2,1,0:T(8,128)S(1)}, u32[]{:S(2)}, u32[]{:S(2)}) collective-permute-start(f32[2,32,128]{2,1,0:T(8,128)S(1)} %get-tuple-element.121), channel_id=1, source_target_pairs={{0,1},{1,0},{2,3},{3,2},{4,5},{5,4},{6,7},{7,6},{8,9},{9,8},{10,11... | collective-permute-start | bytes 98312 | tf_op jit(solution)/shard_map/ppermute | solution.py:300
  (8 other events, 7.3 us)
